TPU v7x, 512 devices: a whole 4x4x16 slice. The times are simulated.
512 devices in a mesh: pipe: 2 (over z_hi), ctx: 64 (over y, z_lo, core), tp: 4 (over x).
Axes of the slice: x: 4, y: 4, z: 16 (z_hi: 2, z_lo: 8; z = z_hi * 8 + z_lo), core: 2. Of those that a mesh axis runs over, the one named last changes fastest.
Arguments:
- section_output: bfloat16 [2, 8192, 8192], P('pipe', 'ctx', 'tp'), may hold values from -26 to 26
- norm_gain: float32 [2, 8192], P('pipe'), may hold values from 0.1 to 1.9
- kv_weight: bfloat16 [2, 8192, 1024], P('pipe', 'ctx', 'tp'), may hold values from -0.0625 to 0.0625
- queries: bfloat16 [2, 8192, 4096], P('pipe', 'ctx', 'tp'), may hold values from -171 to 171
- rank_block: int32 [128], replicated, may hold values from 0 to 127, each once
Outputs:
- attention: bfloat16 [2, 8192, 4096], P('pipe', 'ctx', 'tp')
- log_total: float32 [2, 8192, 32], P('pipe', 'ctx', 'tp')
Inputs may be any that keep to these rules, and one draw needn't show every extreme that they name: `rank_block`: each of 0 to 127 once.
All inputs are finite; a program needn't handle non-finite values.
Results may differ from a plain program's by a relative error of at most 0.017.
The roundings to bfloat16 on the way count: a program that leaves them out, or rounds other values in their place, can miss the bound.
Values may be sent and summed in bfloat16 or wider, within the bound.
No kernel may reach another device: no remote copies, remote signals or barrier semaphores. Data moves between devices by JAX's collectives and lax.ppermute only.
A program may use at most 128 MiB of HBM per device.

v0:
```python
import math
import jax
import jax.numpy as jnp
from jax import lax
from jax.sharding import PartitionSpec as P

HD = 128
norm_eps = 1e-05
rope_base = 500000.0
mask_fill = -1e30


def passed_along(shard, axis, by):
    peers = lax.axis_size(axis)
    return lax.ppermute(shard, axis, [(i, (i + by) % peers) for i in range(peers)])


def block_positions(rank_block, ctx_count, half_rows):
    block_ids = rank_block.reshape(ctx_count, 2)
    within = jnp.arange(half_rows, dtype=jnp.int32)
    return (block_ids[:, :, None] * half_rows + within[None, None, :]).reshape(-1)


def rotate_keys(raw_keys, positions):
    width = raw_keys.shape[-1]
    half_width = width // 2
    steps_f = jnp.arange(half_width, dtype=jnp.float32)
    inv_freq = jnp.exp(steps_f * (-2.0 / width) * math.log(rope_base))
    angles = positions.astype(jnp.float32)[:, None] * inv_freq[None, :]
    cosine = jnp.cos(angles)
    sine_part = jnp.sin(angles)
    first_half = raw_keys[:, :half_width]
    second_half = raw_keys[:, half_width:]
    return jnp.concatenate(
        [
            first_half * cosine - second_half * sine_part,
            second_half * cosine + first_half * sine_part,
        ],
        axis=1,
    )


def body(section_output, norm_gain, kv_weight, queries, rank_block):
    ctx_count = lax.axis_size("ctx")
    tok_rows = section_output.shape[1]
    half_rows = tok_rows // 2
    head_dim = HD
    head_count = queries.shape[2] // head_dim
    score_scale = 1.0 / math.sqrt(head_dim)
    received = passed_along(section_output, "pipe", 1)
    gathered = lax.all_gather(received, "tp", axis=2, tiled=True)[0].astype(jnp.float32)
    mean_sq = jnp.mean(gathered * gathered, axis=-1, keepdims=True)
    normed = (gathered * lax.rsqrt(mean_sq + norm_eps) * norm_gain[0]).astype(jnp.bfloat16)
    projected = jnp.dot(
        normed,
        lax.all_gather(kv_weight, "ctx", axis=1, tiled=True)[0],
        preferred_element_type=jnp.float32,
    )
    all_pos = block_positions(rank_block, ctx_count, half_rows)
    own_pos = lax.dynamic_slice_in_dim(all_pos, lax.axis_index("ctx") * tok_rows, tok_rows)
    keys = rotate_keys(projected[:, :head_dim], own_pos).astype(jnp.bfloat16)
    values = projected[:, head_dim:].astype(jnp.bfloat16)
    key_values = jnp.concatenate([keys, values], axis=1)
    query_rows = queries[0].reshape(tok_rows, head_count, head_dim)
    halves = (
        (query_rows[:half_rows], own_pos[:half_rows]),
        (query_rows[half_rows:], own_pos[half_rows:]),
    )

    def tile_logits(query_part, query_pos, segment, key_pos):
        logits = (
            jnp.einsum(
                "qhd,kd->hqk", query_part, segment[:, :head_dim], preferred_element_type=jnp.float32
            )
            * score_scale
        )
        allowed = key_pos[None, None, :] <= query_pos[None, :, None]
        return (logits, allowed)

    def weighted_sum(att_weights, segment):
        return jnp.einsum(
            "hqk,kd->qhd",
            att_weights,
            segment[:, head_dim:].astype(jnp.float32),
            precision=lax.Precision.HIGHEST,
        )

    start_pair = (
        jnp.full((head_count, half_rows), mask_fill, jnp.float32),
        jnp.zeros((head_count, half_rows), jnp.float32),
    )
    init_totals = (start_pair, start_pair)
    start_accum = jnp.zeros((half_rows, head_count, head_dim), jnp.float32)
    init_outputs = (start_accum, start_accum)
    segment = lax.all_gather(key_values, "ctx", axis=0, tiled=True)
    key_pos = all_pos
    results = []
    for half_idx in range(2):
        query_part, query_pos = halves[half_idx]

        def update(state_in, query_part=query_part, query_pos=query_pos):
            logits, allowed = tile_logits(query_part, query_pos, segment, key_pos)
            logits = jnp.where(allowed, logits, mask_fill)
            row_max = jnp.maximum(state_in[0], jnp.max(logits, axis=-1))
            row_sum = jnp.sum(jnp.exp(logits - row_max[..., None]), axis=-1)
            return (row_max, row_sum)

        results.append(update(init_totals[half_idx]))
    totals = tuple(results)
    log_halves = tuple((running_pair[0] + jnp.log(running_pair[1]) for running_pair in totals))
    output_segment = lax.all_gather(key_values, "ctx", axis=0, tiled=True)
    results = []
    for half_idx in range(2):
        query_part, query_pos = halves[half_idx]
        log_half = log_halves[half_idx]

        def update(accum, query_part=query_part, query_pos=query_pos, log_half=log_half):
            logits, allowed = tile_logits(query_part, query_pos, output_segment, all_pos)
            att_weights = jnp.where(allowed, jnp.exp(logits - log_half[..., None]), 0.0)
            return weighted_sum(att_weights, output_segment)

        results.append(update(init_outputs[half_idx]))
    outputs = tuple(results)
    attention = (
        jnp.concatenate(outputs, axis=0)
        .astype(jnp.bfloat16)
        .reshape(tok_rows, head_count * head_dim)
    )
    log_total = jnp.concatenate(
        [jnp.transpose(log_halves[0]), jnp.transpose(log_halves[1])], axis=0
    )
    return (attention[None], log_total[None])


def solution(mesh):
    return jax.shard_map(
        body,
        mesh=mesh,
        in_specs=(
            P("pipe", "ctx", "tp"),
            P("pipe", None),
            P("pipe", "ctx", "tp"),
            P("pipe", "ctx", "tp"),
            P(),
        ),
        out_specs=(P("pipe", "ctx", "tp"), P("pipe", "ctx", "tp")),
        check_vma=False,
    )
```

profile of v0, /device:TPU:1, one launch (start us, length us, event | category | flops | bytes accessed | tf_op | source)
XLA Modules:
  0.0 424.6 jit_solution(8950425790996297745)
XLA Ops:
  7.2 16.3 %collective-permute-start = (bf16[1,128,2048]{2,1,0:T(8,128)(2,1)}, bf16[1,128,2048]{2,1,0:T(8,128)(2,1)S(1)}, u32[]{:S(2)}, u32[]{:S(2)}) collective-permute-start(bf16[1,128,2048]{2,1,0:T(8,128)(2,1)} %param.5), channel_id=1, source_target_pairs={{0,256},{256,0},{1,257},{257,1},{2,258},{258,2},{3,259},{259,3},{4... | collective-permute-start | bytes 1572872 | tf_op jit(solution)/shard_map/ppermute | solution.py:15
  23.5 15.2 %collective-permute-done = bf16[1,128,2048]{2,1,0:T(8,128)(2,1)S(1)} collective-permute-done((bf16[1,128,2048]{2,1,0:T(8,128)(2,1)}, bf16[1,128,2048]{2,1,0:T(8,128)(2,1)S(1)}, u32[]{:S(2)}, u32[]{:S(2)}) %collective-permute-start) | collective-permute-done | bytes 524320 | tf_op jit(solution)/shard_map/ppermute | solution.py:15
  38.7 0.8 copy-done.1
  39.6 0.7 all-gather.6.cloned.1.call-update
  40.3 0.7 broadcast_multiply_fusion
  41.0 0.1 mul.100
  41.1 0.1 iota_add_fusion
  41.3 0.1 add.65
  41.4 0.1 fusion.57
  41.5 68.4 %all-gather.4.cloned.1.call-done = bf16[1,128,8192]{2,1,0:T(8,128)(2,1)} async-done(((bf16[1,128,2048]{2,1,0:T(8,128)(2,1)}), bf16[1,128,8192]{2,1,0:T(8,128)(2,1)}) %all-gather.4.cloned.1.call-update) | async-done | bytes 2097168 | tf_op jit(solution)/shard_map/all_gather | solution.py:51
  109.8 2.1 fusion.20
  111.9 123.5 %all-gather.6.cloned.1.call-done = bf16[1,8192,256]{2,1,0:T(8,128)(2,1)} async-done(((bf16[1,128,256]{2,1,0:T(8,128)(2,1)}), bf16[1,8192,256]{2,1,0:T(8,128)(2,1)}) %all-gather.6.cloned.1.call-update) | async-done | bytes 4194320 | tf_op jit(solution)/shard_map/all_gather | solution.py:56
  235.4 3.6 fusion.23
  239.0 0.1 fusion.58
  239.2 0.1 copy.19
  239.3 0.2 fusion.50
  239.5 0.1 copy.13
  239.6 0.1 copy.14
  239.7 0.7 pad_maximum_fusion.1
  240.5 1.0 slice_bitcast_fusion.15
  241.5 0.1 fusion.59
  241.6 0.6 broadcast_compare_fusion.1
  242.3 116.9 %all-gather.8.cloned.1.call-done = bf16[8192,256]{1,0:T(8,128)(2,1)} async-done(((bf16[128,256]{1,0:T(8,128)(2,1)}), bf16[8192,256]{1,0:T(8,128)(2,1)}) %all-gather.8.cloned.1.call-update) | async-done | bytes 4194320 | tf_op jit(solution)/shard_map/all_gather | solution.py:111
  359.2 9.1 %fusion.8 = (f32[8,64]{1,0:T(8,128)S(1)}, f32[8192,64,8]{0,1,2:T(8,128)}) fusion(pred[64,8192]{1,0:T(8,128)(4,1)S(1)} %get-tuple-element.10, bf16[64,8,128]{2,1,0:T(8,128)(2,1)S(1)} %bitcast.76, bf16[8192,256]{1,0:T(8,128)(2,1)} %all-gather.8.cloned.1.call-done), kind=kOutput, calls=%fused_computation.12 | convolution fusion | flops 1086324224 | bytes 19531776 | tf_op jit(solution)/shard_map/qhd,kd->hqk/dot_general | solution.py:72
  368.3 3.1 fusion.9
  371.4 16.4 %exponential_reduce_fusion = (f32[8,64]{1,0:T(8,128)S(1)}, f32[8,64]{1,0:T(8,128)S(1)}) fusion(f32[8192,64,8]{0,1,2:T(8,128)S(1)} %get-tuple-element.15, f32[8,64]{1,0:T(8,128)S(1)} %broadcast_maximum_fusion, pred[64,8192]{1,0:T(8,128)(4,1)S(1)} %get-tuple-element.11, f32[8,64]{1,0:T(8,128)S(1)} %broadcast_maximum_fusion.1, ...), kind=kLoop, calls=%fused_computation.10 | loop fusion | flops 33553408 | bytes 34611200 | tf_op jit(solution)/shard_map/reduce_sum | solution.py:105
  387.8 14.0 %fusion.40 = bf16[64,8,128]{2,0,1:T(8,128)(2,1)S(1)} fusion(f32[8192,64,8]{0,1,2:T(8,128)} %get-tuple-element.17, f32[8,64]{1,0:T(8,128)S(1)} %log_add_fusion.1, pred[64,8192]{1,0:T(8,128)(4,1)S(1)} %get-tuple-element.10, bf16[8192,256]{1,0:T(8,128)(2,1)S(1)} %copy-done.2), kind=kOutput, calls=%fused_computation.41 | convolution fusion | flops 6455099392 | bytes 19533824 | tf_op jit(solution)/shard_map/hqk,kd->qhd/dot_general | solution.py:81
  401.9 0.1 copy.16
  402.1 14.4 %fusion.37 = bf16[64,8,128]{2,0,1:T(8,128)(2,1)S(1)} fusion(f32[8192,64,8]{0,1,2:T(8,128)} %copy-done, f32[8,64]{1,0:T(8,128)S(1)} %log_add_fusion, pred[64,8192]{1,0:T(8,128)(4,1)S(1)} %get-tuple-element.11, bf16[8192,256]{1,0:T(8,128)(2,1)} %all-gather.8.cloned.1.call-done), kind=kOutput, calls=%fused_computation.40 | convolution fusion | flops 6455099392 | bytes 19531776 | tf_op jit(solution)/shard_map/hqk,kd->qhd/dot_general | solution.py:81
  416.5 0.1 copy.18
  416.7 0.7 pad_maximum_fusion
  417.4 0.7 maximum_bitcast_fusion
  (22 shorter events, 0.4 us)
Async XLA Ops:
  7.2 102.7 %all-gather.4.cloned.1.call-start = ((), (), s32[]{:S(2)}) async-start(), calls=%async_computation | async-start | bytes 2621440 | tf_op jit(solution)/shard_map/all_gather | solution.py:51
  7.2 31.5 %collective-permute-start = (bf16[1,128,2048]{2,1,0:T(8,128)(2,1)}, bf16[1,128,2048]{2,1,0:T(8,128)(2,1)S(1)}, u32[]{:S(2)}, u32[]{:S(2)}) collective-permute-start(bf16[1,128,2048]{2,1,0:T(8,128)(2,1)} %param.5), channel_id=1, source_target_pairs={{0,256},{256,0},{1,257},{257,1},{2,258},{258,2},{3,259},{259,3},{4... | collective-permute-start | bytes 1572872 | tf_op jit(solution)/shard_map/ppermute | solution.py:15
  38.7 0.8 copy-start.1
  39.5 195.9 %all-gather.6.cloned.1.call-start = ((), (), s32[]{:S(2)}) async-start(), calls=%async_computation.1 | async-start | bytes 4259840 | tf_op jit(solution)/shard_map/all_gather | solution.py:56
  40.3 318.9 %all-gather.8.cloned.1.call-start = ((), (), s32[]{:S(2)}) async-start(), calls=%async_computation.2 | async-start | bytes 4259840 | tf_op jit(solution)/shard_map/all_gather | solution.py:111
  359.2 9.1 %copy-start.2 = (bf16[8192,256]{1,0:T(8,128)(2,1)S(1)}, bf16[8192,256]{1,0:T(8,128)(2,1)}, u32[]{:S(2)}) copy-start(bf16[8192,256]{1,0:T(8,128)(2,1)} %all-gather.8.cloned.1.call-done) | copy-start | bytes 12582916
  371.4 16.4 %copy-start = (f32[8192,64,8]{0,1,2:T(8,128)}, f32[8192,64,8]{0,1,2:T(8,128)S(1)}, u32[]{:S(2)}) copy-start(f32[8192,64,8]{0,1,2:T(8,128)S(1)} %get-tuple-element.15) | copy-start | bytes 50331652
Sparse Core Ops, SparseCore 0:
  39.7 70.1 all-gather.3
  112.0 123.3 all-gather.5
  240.6 118.5 all-gather.7
where the time goes:
time: 425 us
  waiting for transfers between devices  325 us (76%)
  matrix products  44.3 us (10%)
  other arithmetic  22.4 us (5%)
  starting transfers between devices  16.4 us (4%)
  between operations  13.9 us (3%)
    all_gather x1, waiting for transfers between devices, body(): lax.all_gather(kv_weight, 'ctx', axis=1, tiled=True)[0]  123 us
    all_gather x1, waiting for transfers between devices, body(): output_segment = lax.all_gather(key_values, 'ctx', axis=0, tiled=True)  117 us
    all_gather x1, waiting for transfers between devices, body(): lax.all_gather(received, 'tp', axis=2, tiled=True)[0].astype(jnp.float32)  68.4 us
    dot_general x2, matrix products, weighted_sum(): jnp.einsum('hqk,kd->qhd', att_weights, segment[:, head_dim:].astype(jnp.f...  28.5 us
    reduce_sum x1, other arithmetic, update(): row_sum = jnp.sum(jnp.exp(logits - row_max[..., None]), axis=-1)  16.4 us
    ppermute x1, starting transfers between devices, passed_along(): lax.ppermute(shard, axis, [(i, (i + by) % peers) for i in range(peers)])  16.3 us
    ppermute x1, waiting for transfers between devices, passed_along(): lax.ppermute(shard, axis, [(i, (i + by) % peers) for i in range(peers)])  15.2 us
    dot_general x2, matrix products, tile_logits(): jnp.einsum('qhd,kd->hqk', query_part, segment[:, :head_dim], preferred_el...  12.2 us
  transfers between devices with their start and end apart: 4, of which 4 were waited for; matrix products, arithmetic and copies ran while one was open for 1% of the time, Pallas kernels for 0%

commit v1 on v0

--- a/solution.py
+++ b/solution.py
@@ -53,7 +53,9 @@
     normed = (gathered * lax.rsqrt(mean_sq + norm_eps) * norm_gain[0]).astype(jnp.bfloat16)
     projected = jnp.dot(
         normed,
-        lax.all_gather(kv_weight, "ctx", axis=1, tiled=True)[0],
+        jnp.concatenate(
+            lax.all_to_all(jnp.stack([kv_weight] * lax.axis_size("ctx")), "ctx", 0, 0), axis=1
+        )[0],
         preferred_element_type=jnp.float32,
     )
     all_pos = block_positions(rank_block, ctx_count, half_rows)

time: 425 us -> 480 us (1.13)
  waiting for transfers between devices: 325 us -> 369 us
  starting transfers between devices: 16.4 us -> 25.4 us
    all_gather x1 -> x0, waiting for transfers between devices: 123 us -> none  [body(): lax.all_gather(kv_weight, 'ctx', axis=1, tiled=True)[0]]
    ppermute x1, waiting for transfers between devices: 15.2 us -> 99.9 us  [passed_along(): lax.ppermute(shard, axis, [(i, (i + by) % peers) for i in range(peers)])]
    all_gather x1, waiting for transfers between devices: 68.4 us -> 147 us  [body(): lax.all_gather(received, 'tp', axis=2, tiled=True)[0].astype(jnp.float32)]
    all_to_all x0 -> x1, starting transfers between devices: none -> 17.4 us  [body(): lax.all_to_all(jnp.stack([kv_weight] * lax.axis_size('ctx')), 'ctx', 0, 0)]
    ppermute x1, starting transfers between devices: 16.3 us -> 7.94 us  [passed_along(): lax.ppermute(shard, axis, [(i, (i + by) % peers) for i in range(peers)])]
    all_gather x1, waiting for transfers between devices: 117 us -> 123 us  [body(): output_segment = lax.all_gather(key_values, 'ctx', axis=0, tiled=True)]
  transfers between devices with their start and end apart: 4 -> 4, of which waited for: 4 -> 3; matrix products, arithmetic and copies ran while one was open for 1% -> 1% of each run, Pallas kernels for 0% -> 0%
where the time goes in v1:
time: 480 us
  waiting for transfers between devices  369 us (77%)
  matrix products  44.8 us (9%)
  starting transfers between devices  25.4 us (5%)
  other arithmetic  20.5 us (4%)
  between operations  14.3 us (3%)
  local copies, waits for them, and re-layouts  5.35 us (1%)
    all_gather x1, waiting for transfers between devices, body(): lax.all_gather(received, 'tp', axis=2, tiled=True)[0].astype(jnp.float32)  147 us
    all_gather x1, waiting for transfers between devices, body(): output_segment = lax.all_gather(key_values, 'ctx', axis=0, tiled=True)  123 us
    ppermute x1, waiting for transfers between devices, passed_along(): lax.ppermute(shard, axis, [(i, (i + by) % peers) for i in range(peers)])  99.9 us
    dot_general x2, matrix products, weighted_sum(): jnp.einsum('hqk,kd->qhd', att_weights, segment[:, head_dim:].astype(jnp.f...  28.7 us
    all_to_all x1, starting transfers between devices, body(): lax.all_to_all(jnp.stack([kv_weight] * lax.axis_size('ctx')), 'ctx', 0, 0)  17.4 us
    reduce_sum x1, other arithmetic, update(): row_sum = jnp.sum(jnp.exp(logits - row_max[..., None]), axis=-1)  14.6 us
    dot_general x2, matrix products, tile_logits(): jnp.einsum('qhd,kd->hqk', query_part, segment[:, :head_dim], preferred_el...  12.6 us
  transfers between devices with their start and end apart: 4, of which 3 were waited for; matrix products, arithmetic and copies ran while one was open for 1% of the time, Pallas kernels for 0%

profile of v1, /device:TPU:1, one launch (start us, length us, event | category | flops | bytes accessed | tf_op | source)
XLA Modules:
  0.0 479.8 jit_solution(7184379556581599710)
XLA Ops:
  7.2 3.4 stack.2
  10.5 17.4 %all-to-all-start = ((bf16[64,1,128,256]{3,2,1,0:T(8,128)(2,1)}), bf16[64,1,128,256]{3,2,1,0:T(8,128)(2,1)}, u32[]{:S(2)}, u32[]{:S(2)}) async-start(bf16[64,1,128,256]{3,2,1,0:T(8,128)(2,1)} %stack.2), calls=%async_computation | async-start | bytes 8388608 | tf_op jit(solution)/shard_map/all_to_all | solution.py:57
  28.0 7.9 %collective-permute-start = (bf16[1,128,2048]{2,1,0:T(8,128)(2,1)}, bf16[1,128,2048]{2,1,0:T(8,128)(2,1)S(1)}, u32[]{:S(2)}, u32[]{:S(2)}) collective-permute-start(bf16[1,128,2048]{2,1,0:T(8,128)(2,1)} %param.5), channel_id=1, source_target_pairs={{0,256},{256,0},{1,257},{257,1},{2,258},{258,2},{3,259},{259,3},{4... | collective-permute-start | bytes 1572872 | tf_op jit(solution)/shard_map/ppermute | solution.py:15
  36.0 99.9 %collective-permute-done = bf16[1,128,2048]{2,1,0:T(8,128)(2,1)S(1)} collective-permute-done((bf16[1,128,2048]{2,1,0:T(8,128)(2,1)}, bf16[1,128,2048]{2,1,0:T(8,128)(2,1)S(1)}, u32[]{:S(2)}, u32[]{:S(2)}) %collective-permute-start) | collective-permute-done | bytes 524320 | tf_op jit(solution)/shard_map/ppermute | solution.py:15
  135.8 0.8 copy-done.1
  136.7 0.7 broadcast_multiply_fusion
  137.4 0.1 mul.100
  137.5 0.1 iota_add_fusion
  137.7 0.1 add.65
  137.8 0.1 fusion.56
  137.9 146.8 %all-gather.3.cloned.1.call-done = bf16[1,128,8192]{2,1,0:T(8,128)(2,1)} async-done(((bf16[1,128,2048]{2,1,0:T(8,128)(2,1)}), bf16[1,128,8192]{2,1,0:T(8,128)(2,1)}) %all-gather.3.cloned.1.call-update) | async-done | bytes 2097168 | tf_op jit(solution)/shard_map/all_gather | solution.py:51
  284.7 2.1 fusion.20
  286.8 3.6 fusion.24
  290.4 0.1 fusion.57
  290.5 0.1 copy.20
  290.5 0.1 copy.19
  290.6 0.2 fusion.49
  290.9 0.1 copy.13
  291.0 0.1 copy.14
  291.1 0.7 pad_maximum_fusion.1
  291.9 0.1 fusion.58
  292.0 0.6 broadcast_compare_fusion.1
  292.7 122.7 %all-gather.5.cloned.1.call-done = bf16[8192,256]{1,0:T(8,128)(2,1)} async-done(((bf16[128,256]{1,0:T(8,128)(2,1)}), bf16[8192,256]{1,0:T(8,128)(2,1)}) %all-gather.5.cloned.1.call-update) | async-done | bytes 4194320 | tf_op jit(solution)/shard_map/all_gather | solution.py:113
  415.4 4.8 fusion.9
  420.2 7.8 %fusion.8 = (f32[8,64]{1,0:T(8,128)S(1)}, f32[8192,64,8]{0,1,2:T(8,128)}) fusion(pred[64,8192]{1,0:T(8,128)(4,1)S(1)} %get-tuple-element.10, bf16[64,8,128]{2,1,0:T(8,128)(2,1)S(1)} %bitcast.75, bf16[8192,256]{1,0:T(8,128)(2,1)S(1)} %copy-done.3), kind=kOutput, calls=%fused_computation.12 | convolution fusion | flops 1086324224 | bytes 19531776 | tf_op jit(solution)/shard_map/qhd,kd->hqk/dot_general | solution.py:74
  428.0 14.6 %exponential_reduce_fusion = (f32[8,64]{1,0:T(8,128)S(1)}, f32[8,64]{1,0:T(8,128)S(1)}) fusion(f32[8192,64,8]{0,1,2:T(8,128)S(1)} %get-tuple-element.15, f32[8,64]{1,0:T(8,128)S(1)} %broadcast_maximum_fusion, pred[64,8192]{1,0:T(8,128)(4,1)S(1)} %get-tuple-element.11, f32[8,64]{1,0:T(8,128)S(1)} %broadcast_maximum_fusion.1, ...), kind=kLoop, calls=%fused_computation.10 | loop fusion | flops 33553408 | bytes 34611200 | tf_op jit(solution)/shard_map/reduce_sum | solution.py:107
  442.6 14.0 %fusion.39 = bf16[64,8,128]{2,0,1:T(8,128)(2,1)S(1)} fusion(f32[8192,64,8]{0,1,2:T(8,128)} %get-tuple-element.17, f32[8,64]{1,0:T(8,128)S(1)} %log_add_fusion.1, pred[64,8192]{1,0:T(8,128)(4,1)S(1)} %get-tuple-element.10, bf16[8192,256]{1,0:T(8,128)(2,1)S(1)} %copy-done.3), kind=kOutput, calls=%fused_computation.40 | convolution fusion | flops 6455099392 | bytes 19533824 | tf_op jit(solution)/shard_map/hqk,kd->qhd/dot_general | solution.py:83
  456.6 0.1 copy.16
  456.8 14.7 %fusion.36 = bf16[64,8,128]{2,0,1:T(8,128)(2,1)S(1)} fusion(f32[8192,64,8]{0,1,2:T(8,128)} %copy-done, f32[8,64]{1,0:T(8,128)S(1)} %log_add_fusion, pred[64,8192]{1,0:T(8,128)(4,1)S(1)} %get-tuple-element.11, bf16[8192,256]{1,0:T(8,128)(2,1)} %all-gather.5.cloned.1.call-done), kind=kOutput, calls=%fused_computation.39 | convolution fusion | flops 6455099392 | bytes 19531776 | tf_op jit(solution)/shard_map/hqk,kd->qhd/dot_general | solution.py:83
  471.4 0.1 copy.18
  471.6 0.7 pad_maximum_fusion
  472.3 0.7 maximum_bitcast_fusion
  (24 shorter events, 0.4 us)
Async XLA Ops:
  7.2 284.7 %copy-start.2 = (bf16[1,128,1024]{2,1,0:T(8,128)(2,1)S(1)}, bf16[1,128,1024]{2,1,0:T(8,128)(2,1)}, u32[]{:S(2)}) copy-start(bf16[1,128,1024]{2,1,0:T(8,128)(2,1)} %param.8) | copy-start | bytes 786436
  10.5 276.2 %all-to-all-start = ((bf16[64,1,128,256]{3,2,1,0:T(8,128)(2,1)}), bf16[64,1,128,256]{3,2,1,0:T(8,128)(2,1)}, u32[]{:S(2)}, u32[]{:S(2)}) async-start(bf16[64,1,128,256]{3,2,1,0:T(8,128)(2,1)} %stack.2), calls=%async_computation | async-start | bytes 8388608 | tf_op jit(solution)/shard_map/all_to_all | solution.py:57
  28.0 256.7 %all-gather.3.cloned.1.call-start = ((), (), s32[]{:S(2)}) async-start(), calls=%async_computation.1 | async-start | bytes 2621440 | tf_op jit(solution)/shard_map/all_gather | solution.py:51
  28.0 107.8 %collective-permute-start = (bf16[1,128,2048]{2,1,0:T(8,128)(2,1)}, bf16[1,128,2048]{2,1,0:T(8,128)(2,1)S(1)}, u32[]{:S(2)}, u32[]{:S(2)}) collective-permute-start(bf16[1,128,2048]{2,1,0:T(8,128)(2,1)} %param.5), channel_id=1, source_target_pairs={{0,256},{256,0},{1,257},{257,1},{2,258},{258,2},{3,259},{259,3},{4... | collective-permute-start | bytes 1572872 | tf_op jit(solution)/shard_map/ppermute | solution.py:15
  135.8 0.8 copy-start.1
  136.7 278.7 %all-gather.5.cloned.1.call-start = ((), (), s32[]{:S(2)}) async-start(), calls=%async_computation.2 | async-start | bytes 4259840 | tf_op jit(solution)/shard_map/all_gather | solution.py:113
  415.4 4.8 copy-start.3
  420.2 22.4 %copy-start = (f32[8192,64,8]{0,1,2:T(8,128)}, f32[8192,64,8]{0,1,2:T(8,128)S(1)}, u32[]{:S(2)}) copy-start(f32[8192,64,8]{0,1,2:T(8,128)S(1)} %get-tuple-element.15) | copy-start | bytes 50331652
Sparse Core Ops, SparseCore 0:
  136.8 147.8 all-gather.2
  292.0 123.3 all-gather.4
